TPU v7x, 256 devices: a whole 4x4x8 slice. The times are simulated.
256 devices in a mesh: group: 8 (over z), block: 32 (over x, y, core).
Axes of the slice: x: 4, y: 4, z: 8, core: 2. Of those that a mesh axis runs over, the one named last changes fastest.
Arguments:
- jacobians: bfloat16 [3072, 128, 1152], P(('group', 'block')), may hold values from -0.15625 to 0.15625
- destination: int32 [3072], P(('group', 'block')), may hold values from 0 to 31, as said below
- other_group: int32 [3072], P(('group', 'block')), may hold values from 0 to 7, as said below
- live_rows: int32 [3072], P(('group', 'block')), may hold values from 64 to 128, as said below
- damping: float32 [256, 576], P(('group', 'block')), may hold values from 0.5 to 2
- right_side: float32 [256, 576], P(('group', 'block')), may hold values from -18 to 18
Outputs:
- solution: float32 [256, 576], P(('group', 'block'))
- residual: float32 [256, 576], P(('group', 'block'))
Inputs may be any that keep to these rules, and one draw needn't show every extreme that they name: `destination`: the observation blocks of one device name any one camera block at most 2 times; in every group some camera block is named exactly 2 times by every device of that group. `other_group`: an observation block's covisible group differs from the group of the device that holds it. `live_rows`: every device holds a block whose 128 rows are all live.
All inputs are finite; a program needn't handle non-finite values.
Results may differ from a plain program's by a relative error of at most 0.009.
Values may be sent and summed in bfloat16 or wider, within the bound.
A program may use at most 128 MiB of HBM per device.

v0:
```python
import jax
import jax.numpy as jnp
from jax import lax
from jax.sharding import PartitionSpec as P

ITERS = 2


def global_norm(residual, scaled_res):
    return lax.psum(jnp.sum(residual * scaled_res), ("group", "block"))


def on_device(jacobians, destination, other_group, live_rows, damping, right_side):
    block_count, row_count, block_width = jacobians.shape
    param_count = block_width // 2
    owners = lax.axis_size("block")
    groups = lax.axis_size("group")
    my_group = lax.axis_index("group")
    row_index = jnp.arange(row_count, dtype=jnp.int32)
    kept_blocks = jnp.where(
        row_index[None, :, None] < live_rows[:, None, None], jacobians, jnp.zeros_like(jacobians)
    )
    capacity = max(2, 2 * ((block_count + owners - 1) // owners))
    same_owner = destination[:, None] == destination[None, :]
    positions = jnp.arange(block_count, dtype=jnp.int32)
    before = positions[None, :] < positions[:, None]
    slot_rank = jnp.sum((same_owner & before).astype(jnp.int32), axis=1)
    slot_index = destination * capacity + slot_rank
    send_blocks = (
        jnp.zeros((owners * capacity, row_count, block_width), jnp.bfloat16)
        .at[slot_index]
        .set(kept_blocks)
    )
    send_groups = jnp.zeros((owners * capacity,), jnp.int32).at[slot_index].set(other_group)
    send_blocks = send_blocks.reshape(owners, capacity, row_count, block_width)
    send_groups = send_groups.reshape(owners, capacity)
    got_blocks, got_groups = (
        lax.all_to_all(send_blocks, "block", split_axis=0, concat_axis=0, tiled=True),
        lax.all_to_all(send_groups, "block", split_axis=0, concat_axis=0, tiled=True),
    )
    got_blocks = got_blocks.reshape(owners * capacity, row_count, block_width)
    got_groups = got_groups.reshape(owners * capacity)
    group_ids = jnp.arange(groups, dtype=jnp.int32)
    own_mask = (group_ids == my_group).astype(jnp.float32)
    selector = (got_groups[:, None] == group_ids[None, :]).astype(jnp.float32)
    selector_low = selector.astype(jnp.bfloat16)

    def spread(term_rows):
        home_total = jnp.sum(term_rows[:, :param_count], axis=0)
        far_total = jnp.dot(
            selector.T,
            term_rows[:, param_count:],
            precision=lax.Precision.HIGHEST,
            preferred_element_type=jnp.float32,
        )
        return far_total + own_mask[:, None] * home_total[None, :]

    squares = jnp.einsum("src,src->sc", got_blocks, got_blocks, preferred_element_type=jnp.float32)
    diagonal_sum = damping + lax.psum_scatter(
        spread(squares), "group", scatter_dimension=0, tiled=True
    )
    solution = jnp.zeros_like(right_side)
    residual = right_side
    scaled_res = residual / diagonal_sum
    direction = scaled_res
    precond_norm = global_norm(residual, scaled_res)
    for iteration in range(ITERS):
        low_field = direction.astype(jnp.bfloat16)
        panel_low = lax.all_gather(low_field, "group", axis=0, tiled=True)
        far_inputs = jnp.dot(selector_low, panel_low, preferred_element_type=jnp.float32).astype(
            jnp.bfloat16
        )
        near_inputs = jnp.broadcast_to(low_field, far_inputs.shape)
        inputs = jnp.concatenate([near_inputs, far_inputs], axis=1)
        projected = jnp.einsum(
            "src,sc->sr", got_blocks, inputs, preferred_element_type=jnp.float32
        ).astype(jnp.bfloat16)
        returned = jnp.einsum(
            "src,sr->sc", got_blocks, projected, preferred_element_type=jnp.float32
        )
        operator_image = damping * direction + lax.psum_scatter(
            spread(returned), "group", scatter_dimension=0, tiled=True
        )
        curvature = lax.psum(jnp.sum(direction * operator_image), ("group", "block"))
        step_size = precond_norm / curvature
        solution = solution + step_size * direction
        residual = residual - step_size * operator_image
        if iteration + 1 < ITERS:
            scaled_res = residual / diagonal_sum
            next_norm = global_norm(residual, scaled_res)
            direction = scaled_res + next_norm / precond_norm * direction
            precond_norm = next_norm
    return (solution, residual)


def solution(mesh):
    placed = (
        P(("group", "block"), None, None),
        P(("group", "block")),
        P(("group", "block")),
        P(("group", "block")),
        P(("group", "block"), None),
        P(("group", "block"), None),
    )
    return jax.shard_map(
        on_device,
        mesh=mesh,
        in_specs=placed,
        out_specs=(P(("group", "block"), None), P(("group", "block"), None)),
        check_vma=False,
    )
```

profile of v0, /device:TPU:1, one launch (start us, length us, event | category | flops | bytes accessed | tf_op | source)
XLA Modules:
  0.0 751.9 jit_solution(11086218036957085777)
XLA Ops:
  0.6 0.9 convert_reduce_fusion
  1.5 0.7 compare_select_fusion
  2.2 0.7 scatter_custom_fusion
  3.0 0.7 all_to_all.9
  3.7 8.6 %all-to-all-start = ((s32[32,1,2]{2,1,0:T(1,128)}), s32[32,1,2]{2,1,0:T(1,128)S(1)}, u32[]{:S(2)}, u32[]{:S(2)}) async-start(s32[32,1,2]{2,1,0:T(1,128)} %bitcast.2), calls=%async_computation | async-start | bytes 32768 | tf_op jit(solution)/shard_map/all_to_all | solution.py:39
  12.3 0.7 iota_compare_fusion.4
  13.0 2.3 broadcast_select_fusion
  15.3 7.1 broadcast_in_dim.26
  22.4 7.7 %scatter_fusion = bf16[64,128,1152]{2,1,0:T(8,128)(2,1)} fusion(bf16[64,128,1152]{2,1,0:T(8,128)(2,1)} %broadcast_in_dim.26, s32[12]{0:T(128)} %copy-done.2, bf16[12,128,1152]{2,1,0:T(8,128)(2,1)S(1)} %broadcast_select_fusion), kind=kCustom, calls=%fused_computation.1 | custom fusion | bytes 10616880 | tf_op jit(solution)/shard_map/scatter | solution.py:32
  30.2 7.5 all-to-all-start.1
  37.7 0.6 dynamic-slice
  38.3 0.5 broadcast.51
  38.8 0.7 reduce.9
  39.6 261.2 %all-to-all-done.1 = bf16[32,2,128,1152]{3,2,1,0:T(8,128)(2,1)} async-done(((bf16[32,2,128,1152]{3,2,1,0:T(8,128)(2,1)}), bf16[32,2,128,1152]{3,2,1,0:T(8,128)(2,1)}, u32[]{:S(2)}, u32[]{:S(2)}) %all-to-all-start.1) | async-done | bytes 18874400 | tf_op jit(solution)/shard_map/all_to_all | solution.py:38
  300.8 8.3 %fusion = f32[64,1152]{1,0:T(8,128)S(1)} fusion(bf16[32,2,128,1152]{3,2,1,0:T(8,128)(2,1)} %all-to-all-done.1), kind=kLoop, calls=%fused_computation.3 | loop fusion | flops 28237824 | bytes 19169280 | tf_op jit(solution)/shard_map/src,src->sc/dot_general | solution.py:58
  309.4 25.5 %all-reduce = f32[8,576]{1,0:T(8,128)S(1)} all-reduce(f32[8,576]{1,0:T(8,128)S(1)} %convolution_add_fusion.2), channel_id=2, replica_groups=mesh['group'=8,'block'=32] {'group'}, use_global_device_ids=true, to_apply=%region_4.5.clone | all-reduce | flops 4608 | bytes 36864
  334.9 0.7 convert_reduce_fusion.2
  335.5 18.1 %all-gather = bf16[8,1,576]{2,1,0:T(2,128)(2,1)S(1)} all-gather(bf16[1,1,576]{2,1,0:T(2,128)(2,1)S(1)} %convert_bitcast_fusion.3), channel_id=1, replica_groups=mesh['group'=8,'block'=32] {'group'}, dimensions={0}, use_global_device_ids=true | all-gather | bytes 10368 | tf_op jit(solution)/shard_map/all_gather | solution.py:69
  354.0 10.1 %fusion.3 = f32[64,1,128]{2,1,0:T(1,128)S(1)} fusion(bf16[64,128,1152]{2,1,0:T(8,128)(2,1)} %bitcast.4, bf16[64,1152,1]{1,0,2:T(8,128)(2,1)S(1)} %maximum_bitcast_fusion), kind=kOutput, calls=%fused_computation.14 | convolution fusion | flops 18874368 | bytes 19054592 | tf_op jit(solution)/shard_map/src,sc->sr/dot_general | solution.py:75
  364.1 7.8 %fusion.10 = f32[64,1,1152]{2,1,0:T(1,128)S(1)} fusion(bf16[64,128,1152]{2,1,0:T(8,128)(2,1)} %bitcast.4, bf16[64,128,1]{1,0,2:T(8,128)(2,1)S(1)} %convert_bitcast_fusion.1), kind=kOutput, calls=%fused_computation.26 | convolution fusion | flops 18874368 | bytes 19185664 | tf_op jit(solution)/shard_map/src,sr->sc/dot_general | solution.py:78
  372.3 20.1 %all-reduce.1 = f32[8,576]{1,0:T(8,128)S(1)} all-reduce(f32[8,576]{1,0:T(8,128)S(1)} %convolution_add_fusion.1), channel_id=3, replica_groups=mesh['group'=8,'block'=32] {'group'}, use_global_device_ids=true, to_apply=%region_8.9.clone | all-reduce | flops 4608 | bytes 36864
  392.4 1.2 multiply_reduce_fusion.2
  393.7 133.7 %all-reduce.3 = (f32[]{:T(128)}, f32[]{:T(128)}) all-reduce(f32[]{:T(128)} %get-tuple-element.3, f32[]{:T(128)} %get-tuple-element.2), channel_id=1, replica_groups=mesh['group'=8,'block'=32] {'group','block'}, use_global_device_ids=true, to_apply=%region_6.7 | all-reduce | flops 2 | bytes 16 | tf_op jit(solution)/shard_map/psum | solution.py:10
  528.7 1.2 multiply_reduce_fusion.1
  529.9 73.4 %psum.30 = f32[]{:T(128)} all-reduce(f32[]{:T(128)} %get-tuple-element.8), channel_id=1, replica_groups=mesh['group'=8,'block'=32] {'group','block'}, use_global_device_ids=true, to_apply=%region_12.13 | all-reduce | flops 1 | bytes 8 | tf_op jit(solution)/shard_map/psum | solution.py:10
  604.8 17.9 %all-gather.1 = bf16[8,1,576]{2,1,0:T(2,128)(2,1)S(1)} all-gather(bf16[1,1,576]{2,1,0:T(2,128)(2,1)S(1)} %convert_bitcast_fusion.2), channel_id=1, replica_groups=mesh['group'=8,'block'=32] {'group'}, dimensions={0}, use_global_device_ids=true | all-gather | bytes 10368 | tf_op jit(solution)/shard_map/all_gather | solution.py:69
  623.0 10.1 %fusion.1 = f32[64,1,128]{2,1,0:T(1,128)S(1)} fusion(bf16[64,128,1152]{2,1,0:T(8,128)(2,1)} %bitcast.4, bf16[64,1152,1]{1,0,2:T(8,128)(2,1)S(1)} %maximum_bitcast_fusion.1), kind=kOutput, calls=%fused_computation.11 | convolution fusion | flops 18874368 | bytes 19054592 | tf_op jit(solution)/shard_map/src,sc->sr/dot_general | solution.py:75
  633.1 7.8 %fusion.8 = f32[64,1,1152]{2,1,0:T(1,128)S(1)} fusion(bf16[64,128,1152]{2,1,0:T(8,128)(2,1)} %bitcast.4, bf16[64,128,1]{1,0,2:T(8,128)(2,1)S(1)} %convert_bitcast_fusion), kind=kOutput, calls=%fused_computation.24 | convolution fusion | flops 18874368 | bytes 19185664 | tf_op jit(solution)/shard_map/src,sr->sc/dot_general | solution.py:78
  641.3 20.9 %all-reduce.2 = f32[8,576]{1,0:T(8,128)S(1)} all-reduce(f32[8,576]{1,0:T(8,128)S(1)} %convolution_add_fusion), channel_id=4, replica_groups=mesh['group'=8,'block'=32] {'group'}, use_global_device_ids=true, to_apply=%region_14.15.clone | all-reduce | flops 4608 | bytes 36864
  662.3 1.2 multiply_reduce_fusion
  663.5 85.8 %psum.31 = f32[]{:T(128)} all-reduce(f32[]{:T(128)} %multiply_reduce_fusion), channel_id=1, replica_groups=mesh['group'=8,'block'=32] {'group','block'}, use_global_device_ids=true, to_apply=%region_16.17 | all-reduce | flops 1 | bytes 8 | tf_op jit(solution)/shard_map/psum | solution.py:84
  750.6 1.2 multiply_subtract_fusion
  (30 shorter events, 1.8 us)
Async XLA Ops:
  2.2 10.0 %copy-start.2 = (s32[12]{0:T(128)}, s32[12]{0:T(128)S(1)}, u32[]{:S(2)}) copy-start(s32[12]{0:T(128)S(1)} %compare_select_fusion) | copy-start | bytes 148
  3.7 26.5 %all-to-all-start = ((s32[32,1,2]{2,1,0:T(1,128)}), s32[32,1,2]{2,1,0:T(1,128)S(1)}, u32[]{:S(2)}, u32[]{:S(2)}) async-start(s32[32,1,2]{2,1,0:T(1,128)} %bitcast.2), calls=%async_computation | async-start | bytes 32768 | tf_op jit(solution)/shard_map/all_to_all | solution.py:39
  30.2 7.5 %copy-start.3 = (u32[256]{0:T(256)S(1)}, u32[256]{0:T(256)}, u32[]{:S(2)}) copy-start(u32[256]{0:T(256)} %constant.28) | copy-start | bytes 3076
  30.2 270.6 %all-to-all-start.1 = ((bf16[32,2,128,1152]{3,2,1,0:T(8,128)(2,1)}), bf16[32,2,128,1152]{3,2,1,0:T(8,128)(2,1)}, u32[]{:S(2)}, u32[]{:S(2)}) async-start(bf16[32,2,128,1152]{3,2,1,0:T(8,128)(2,1)} %bitcast.41), calls=%async_computation.1 | async-start | bytes 37748736 | tf_op jit(solution)/shard_map/all_to_all | solution.py:38
  37.7 297.2 %copy-start = (f32[1,576]{1,0:T(1,128)S(1)}, f32[1,576]{1,0:T(1,128)}, u32[]{:S(2)}) copy-start(f32[1,576]{1,0:T(1,128)} %param.10) | copy-start | bytes 6916
  37.7 297.2 %copy-start.1 = (f32[1,576]{1,0:T(1,128)S(1)}, f32[1,576]{1,0:T(1,128)}, u32[]{:S(2)}) copy-start(f32[1,576]{1,0:T(1,128)} %param.11) | copy-start | bytes 6916
where the time goes:
time: 753 us; the launch traced here: 752 us
  blocking collectives  396 us (53%)
  waiting for transfers between devices  261 us (35%)
  matrix products  37.2 us (5%)
  other arithmetic  19.4 us (3%)
  local copies, waits for them, and re-layouts  17.6 us (2%)
  starting transfers between devices  16.1 us (2%)
    all_to_all x1, waiting for transfers between devices, on_device(): lax.all_to_all(send_blocks, 'block', split_axis=0, concat_axis=0, tiled=T...  261 us
    psum x2, blocking collectives, global_norm(): return lax.psum(jnp.sum(residual * scaled_res), ('group', 'block'))  207 us
    psum x1, blocking collectives, on_device(): lax.psum(jnp.sum(direction * operator_image), ('group', 'block'))  85.8 us
    unnamed x3, blocking collectives  66.5 us
    all_gather x2, blocking collectives, on_device(): panel_low = lax.all_gather(low_field, 'group', axis=0, tiled=True)  36.1 us
    dot_general x2, matrix products, on_device(): jnp.einsum('src,sc->sr', got_blocks, inputs, preferred_element_type=jnp.f...  20.3 us
    dot_general x2, matrix products, on_device(): jnp.einsum('src,sr->sc', got_blocks, projected, preferred_element_type=jn...  15.7 us
  transfers between devices with their start and end apart: 2, of which 1 were waited for; matrix products, arithmetic and copies ran while one was open for 3% of the time, Pallas kernels for 0%

commit v1 on v0

v1 whole, which is shorter than its diff:
```python
import functools

import jax
import jax.numpy as jnp
from jax import lax
from jax.experimental import pallas as pl
from jax.experimental.pallas import tpu as pltpu
from jax.sharding import PartitionSpec as P

LANES = 128
MSG = 16
F32 = jnp.float32
BF16 = jnp.bfloat16


def total(value):
    return jnp.sum(jnp.sum(value, axis=1, keepdims=True), axis=0, keepdims=True)


def iota(shape, dim):
    return lax.broadcasted_iota(jnp.int32, shape, dim)


def dot(left, right, contract=((1,), (0,))):
    return lax.dot_general(left, right, (contract, ((), ())), preferred_element_type=F32)


def cg_kernel(
    groups, owners, count, rows, params,
    jac_hbm, dest_ref, other_ref, live_ref, damp_ref, rhs_ref,
    sol_ref, res_ref,
    jac, pack, unpack, snd, rcv, ctx, wide, row_snd, row_rcv,
    jac_sem, snd_sem, rcv_sem, zsnd_sem, zrcv_sem,
):
    me_g = lax.axis_index("group")
    me_b = lax.axis_index("block")
    width = jac.shape[1]
    tiles = (params + LANES - 1) // LANES
    padded = tiles * LANES
    kpad = 16

    def block_copy(k):
        part = pl.ds(k * rows, rows)
        return pltpu.make_async_copy(jac_hbm.at[part], jac.at[part], jac_sem.at[k])

    for k in range(count):
        block_copy(k).start()

    barrier = pltpu.get_barrier_semaphore()

    def greet_block(step, carry):
        peer = (me_b + step) % owners
        pl.semaphore_signal(
            barrier, inc=1, device_id=(me_g, peer), device_id_type=pl.DeviceIdType.MESH
        )
        return carry

    def greet_group(step, carry):
        peer = (me_g + step) % groups
        pl.semaphore_signal(
            barrier, inc=1, device_id=(peer, me_b), device_id_type=pl.DeviceIdType.MESH
        )
        return carry

    lax.fori_loop(1, owners, greet_block, 0)
    lax.fori_loop(1, groups, greet_group, 0)

    def own_part():
        return pl.ds(pl.multiple_of(me_b * MSG, MSG), MSG)

    def block_send(stage):
        def body(step, carry):
            peer = (me_b + step) % owners
            pltpu.make_async_remote_copy(
                src_ref=snd.at[stage, pl.ds(pl.multiple_of(peer * MSG, MSG), MSG)],
                dst_ref=rcv.at[stage, own_part()],
                send_sem=snd_sem.at[stage],
                recv_sem=rcv_sem.at[stage],
                device_id=(me_g, peer),
                device_id_type=pl.DeviceIdType.MESH,
            ).start()
            return carry

        lax.fori_loop(1, owners, body, 0)
        rcv[stage, own_part()] = snd[stage, own_part()]

    def block_wait(ref, sem, stage):
        part = ref.at[stage, pl.ds(0, (owners - 1) * MSG)]
        pltpu.make_async_copy(part, part, sem.at[stage]).wait()

    def group_send(stage, src_of, dst):
        def body(step, carry):
            peer = (me_g + step) % groups
            pltpu.make_async_remote_copy(
                src_ref=src_of(peer),
                dst_ref=dst,
                send_sem=zsnd_sem.at[stage],
                recv_sem=zrcv_sem.at[stage],
                device_id=(peer, me_b),
                device_id_type=pl.DeviceIdType.MESH,
            ).start()
            return carry

        lax.fori_loop(1, groups, body, 0)

    def group_wait(part, sem, stage):
        pltpu.make_async_copy(part, part, sem.at[stage]).wait()

    sub = iota((kpad, LANES), 0)
    lane = iota((kpad, LANES), 1)
    dest_col = jnp.full((kpad, LANES), -1, jnp.int32)
    dest_row = jnp.full((kpad, LANES), -1, jnp.int32)
    live_col = jnp.zeros((kpad, LANES), jnp.int32)
    other_col = jnp.zeros((kpad, LANES), jnp.int32)
    for k in range(count):
        dest_col = jnp.where(sub == k, dest_ref[k], dest_col)
        dest_row = jnp.where(lane == k, dest_ref[k], dest_row)
        live_col = jnp.where(sub == k, live_ref[k], live_col)
        other_col = jnp.where(sub == k, other_ref[k], other_col)
    same = jnp.where((dest_col == dest_row) & (dest_row >= 0), 1.0, 0.0)
    rank_row = jnp.sum(jnp.where(sub < lane, same, 0.0), axis=0, keepdims=True)
    rank_col = jnp.sum(jnp.where(lane < sub, same, 0.0), axis=1, keepdims=True)
    slot = iota((3 * owners, LANES), 0)
    dest_rows = jnp.broadcast_to(dest_row[:1], (3 * owners, LANES))
    rank_rows = jnp.broadcast_to(rank_row, (3 * owners, LANES))
    slot_hit = dest_rows == slot % owners
    slot_rank = (slot // owners - 1).astype(F32)
    to_slot = jnp.where(slot_hit & ((slot < owners) | (rank_rows == slot_rank)), 1.0, 0.0)
    to_slot = to_slot[:, :kpad].astype(BF16)
    slot_lane = iota((kpad, LANES), 1)
    lane_hit = dest_col == slot_lane % owners
    lane_rank = (slot_lane // owners - 1).astype(F32)
    rank_cols = jnp.broadcast_to(rank_col, (kpad, LANES))
    from_home = jnp.where(lane_hit & (slot_lane < owners), 1.0, 0.0).astype(BF16)
    from_far = jnp.where(
        lane_hit & (slot_lane >= owners) & (rank_cols == lane_rank), 1.0, 0.0
    ).astype(BF16)
    keep = jnp.concatenate(
        [jnp.where((sub == k) & (lane < live_col), 1.0, 0.0) for k in range(count)], axis=1
    )
    panel_lane = iota((kpad, padded), 1)

    def put_rows(first, value):
        for c in range(tiles):
            pack[pl.ds(first + c, owners, stride=MSG), :] = value[:, c * LANES : (c + 1) * LANES]

    def put_message(stage, home, far_a, far_b, last):
        put_rows(0, home)
        put_rows(tiles, far_a)
        put_rows(2 * tiles, far_b)
        pack[pl.ds(3 * tiles, owners, stride=MSG), :] = last
        snd[stage] = pack[...].astype(BF16)
        block_send(stage)

    def send_terms(stage, terms, last):
        home = jnp.where(panel_lane < params, terms[:, :padded], 0.0)
        far = jnp.where(panel_lane < params, pltpu.roll(terms, params, 1)[:, :padded], 0.0)
        high = home.astype(BF16)
        low = (home - high.astype(F32)).astype(BF16)
        home_out = dot(to_slot[:owners], high) + dot(to_slot[:owners], low)
        far_out = dot(to_slot[owners:], far.astype(BF16))
        put_message(stage, home_out, far_out[:owners], far_out[owners:], last)

    def get_message(stage):
        block_wait(rcv, rcv_sem, stage)
        unpack[...] = rcv[stage].astype(F32)

        def row(c):
            return unpack[pl.ds(c, owners, stride=MSG), :]

        parts = [
            jnp.concatenate([row(s * tiles + c) for c in range(tiles)], axis=1) for s in range(3)
        ]
        return jnp.concatenate(parts, axis=0).astype(BF16), row(3 * tiles)

    last_lane = iota((owners, LANES), 1)

    def split(value, first):
        high = value.astype(BF16).astype(F32)
        middle = (value - high).astype(BF16).astype(F32)
        low = value - high - middle
        out = jnp.where(last_lane == first, jnp.broadcast_to(high, last_lane.shape), 0.0)
        out = out + jnp.where(last_lane == first + 1, jnp.broadcast_to(middle, last_lane.shape), 0.0)
        return out + jnp.where(last_lane == first + 2, jnp.broadcast_to(low, last_lane.shape), 0.0)

    wide_lane = iota((groups, padded), 1)
    wide_row = iota((groups, padded), 0)
    pl.semaphore_wait(barrier, owners - 1 + groups - 1)
    ctx[me_g] = jnp.zeros((2, padded), F32)
    ctx[me_g, 0:1, 0:params] = damp_ref[...]
    ctx[me_g, 1:2, 0:params] = rhs_ref[...]
    group_send(0, lambda peer: ctx.at[me_g], ctx.at[me_g])

    sum_rows = []
    for k in range(count):
        block_copy(k).wait()
        block = jac[k * rows : (k + 1) * rows, :].astype(F32)
        live = iota((rows, width), 0) < live_ref[k]
        kept = jnp.where(live, block, 0.0)
        sum_rows.append(jnp.sum(kept * kept, axis=0, keepdims=True))
    sum_rows += [jnp.zeros((1, width), F32)] * (kpad - count)
    squares = jnp.concatenate(sum_rows, axis=0)
    others = jnp.where(sub < count, other_col, 0).astype(F32).astype(BF16)
    other_out = dot(to_slot[owners:], others)
    send_terms(
        0, squares, jnp.where(last_lane < LANES // 2, other_out[:owners], other_out[owners:])
    )
    got, ids = get_message(0)
    group_col = iota((owners, LANES), 1).astype(F32)
    id_a = jnp.broadcast_to(ids[:, :1], (owners, LANES))
    id_b = jnp.broadcast_to(ids[:, LANES // 2 : LANES // 2 + 1], (owners, LANES))
    select = jnp.concatenate(
        [
            jnp.where(group_col == me_g.astype(F32), 1.0, 0.0),
            jnp.where(group_col == id_a, 1.0, 0.0),
            jnp.where(group_col == id_b, 1.0, 0.0),
        ],
        axis=0,
    )
    if 3 * owners < LANES:
        select_t = jnp.concatenate([select, jnp.zeros((LANES - 3 * owners, LANES), F32)], axis=0).T
    else:
        select_t = select.T
    select = select[:, :kpad].astype(BF16)
    select_t = select_t[:kpad, : 3 * owners].astype(BF16)

    def sum_over_groups(stage, got, scalar):
        panel = dot(select_t, got)[:groups]
        if scalar is not None:
            spot = (wide_row == 0) & (wide_lane == params)
            panel = jnp.where(spot, jnp.broadcast_to(scalar, panel.shape), panel)
        wide[stage, me_g] = panel
        group_send(1 + stage, lambda peer: wide.at[stage, me_g], wide.at[stage, me_g])
        group_wait(wide.at[stage, pl.ds(0, groups - 1)], zrcv_sem, 1 + stage)
        out = wide[stage, 0]
        for g in range(1, groups):
            out = out + wide[stage, g]
        return jnp.where(wide_lane < params, out, 0.0), total(jnp.where(wide_lane < params, 0.0, out))

    def send_panel(stage, panel, last):
        low = jnp.concatenate([panel, jnp.zeros((kpad - groups, padded), F32)], axis=0)
        out = dot(select, low.astype(BF16))
        put_message(stage, out[:owners], out[owners : 2 * owners], out[2 * owners :], last)

    def inputs_of(got):
        home = dot(from_home[:, :owners], got[:owners])
        far = dot(from_far[:, owners : 3 * owners], got[owners:])
        fill = jnp.zeros((kpad, width - padded), F32)
        home = jnp.concatenate([home, fill], axis=1)
        far = pltpu.roll(jnp.concatenate([far, fill], axis=1), params, 1)
        return (home + far).astype(BF16)

    def own_row(panel):
        return jnp.sum(jnp.where(wide_row == me_g, panel, 0.0), axis=0, keepdims=True)

    summed, unused = sum_over_groups(0, got, None)
    group_wait(ctx.at[pl.ds(0, groups - 1)], zrcv_sem, 0)
    damping = jnp.concatenate([ctx[g, 0:1, :] for g in range(groups)], axis=0)
    right_side = jnp.concatenate([ctx[g, 1:2, :] for g in range(groups)], axis=0)
    diagonal = jnp.where(wide_lane < params, damping + summed, 1.0)
    direction = right_side / diagonal

    send_panel(
        1,
        direction,
        split(total(right_side * direction), 0)
        + split(total(damping * direction * direction), LANES // 2),
    )
    got, scalars = get_message(1)
    norm = total(jnp.where(last_lane < LANES // 2, scalars, 0.0))
    damped = total(jnp.where(last_lane < LANES // 2, 0.0, scalars))
    product = dot(inputs_of(got), jac[...], ((1,), (1,)))
    kept = product * keep
    projected = kept.astype(BF16)
    returned = dot(projected, jac[...])
    send_terms(2, returned, split(total(kept * projected.astype(F32)), 0))
    got, scalars = get_message(2)
    summed, square = sum_over_groups(1, got, total(scalars))
    step_size = norm / (damped + square)
    residual = right_side - step_size * (damping * direction + summed)
    scaled = residual / diagonal

    send_panel(3, scaled, split(total(residual * scaled), 0))
    got, scalars = get_message(3)
    next_norm = total(scalars)
    beta = next_norm / norm
    product = dot(inputs_of(got), jac[...], ((1,), (1,))) + beta * product
    kept = product * keep
    projected = kept.astype(BF16)
    returned = dot(projected, jac[...])
    first_direction = own_row(direction)
    own_damping = own_row(damping)
    next_direction = own_row(scaled) + beta * first_direction
    partial = total(kept * projected.astype(F32)) + total(
        own_damping * next_direction * next_direction
    )
    send_terms(4, returned, split(partial, 0))
    got, scalars = get_message(4)
    panel = dot(select_t, got)[:groups]
    panel = jnp.where(wide_lane == params, jnp.broadcast_to(total(scalars), panel.shape), panel)
    for g in range(groups):
        row_snd[g] = panel[g : g + 1]
    row_rcv[me_g] = own_row(panel)
    group_send(3, lambda peer: row_snd.at[peer], row_rcv.at[me_g])
    group_wait(row_rcv.at[pl.ds(0, groups - 1)], zrcv_sem, 3)
    out = row_rcv[0]
    for g in range(1, groups):
        out = out + row_rcv[g]
    one_lane = iota((1, padded), 1)
    curvature = total(jnp.where(one_lane == params, out, 0.0))
    next_step = next_norm / curvature
    image = own_damping * next_direction + out
    sol_ref[...] = (step_size * first_direction + next_step * next_direction)[:, :params]
    res_ref[...] = (own_row(residual) - next_step * image)[:, :params]

    for stage in range(5):
        block_wait(snd, snd_sem, stage)
    group_wait(ctx.at[pl.ds(0, groups - 1)], zsnd_sem, 0)
    for stage in range(2):
        group_wait(wide.at[stage, pl.ds(0, groups - 1)], zsnd_sem, 1 + stage)
    group_wait(row_snd.at[pl.ds(0, groups - 1)], zsnd_sem, 3)


def on_device(groups, owners, jacobians, destination, other_group, live_rows, damping, right_side):
    count, rows, width = jacobians.shape
    params = width // 2
    padded = (params + LANES - 1) // LANES * LANES
    vmem = pl.BlockSpec(memory_space=pltpu.VMEM)
    smem = pl.BlockSpec(memory_space=pltpu.SMEM)
    return pl.pallas_call(
        functools.partial(cg_kernel, groups, owners, count, rows, params),
        out_shape=(
            jax.ShapeDtypeStruct(right_side.shape, F32),
            jax.ShapeDtypeStruct(right_side.shape, F32),
        ),
        in_specs=[pl.BlockSpec(memory_space=pl.ANY), smem, smem, smem, vmem, vmem],
        out_specs=(vmem, vmem),
        scratch_shapes=[
            pltpu.VMEM((count * rows, width), BF16),
            pltpu.VMEM((owners * MSG, LANES), F32),
            pltpu.VMEM((owners * MSG, LANES), F32),
            pltpu.VMEM((5, owners * MSG, LANES), BF16),
            pltpu.VMEM((5, owners * MSG, LANES), BF16),
            pltpu.VMEM((groups, 2, padded), F32),
            pltpu.VMEM((2, groups, groups, padded), F32),
            pltpu.VMEM((groups, 1, padded), F32),
            pltpu.VMEM((groups, 1, padded), F32),
            pltpu.SemaphoreType.DMA((count,)),
            pltpu.SemaphoreType.DMA((5,)),
            pltpu.SemaphoreType.DMA((5,)),
            pltpu.SemaphoreType.DMA((4,)),
            pltpu.SemaphoreType.DMA((4,)),
        ],
        compiler_params=pltpu.CompilerParams(
            collective_id=0, has_side_effects=True, vmem_limit_bytes=40 * 1024 * 1024
        ),
    )(
        jacobians.reshape(count * rows, width), destination, other_group, live_rows, damping, right_side
    )


def solution(mesh):
    placed = (
        P(("group", "block"), None, None),
        P(("group", "block")),
        P(("group", "block")),
        P(("group", "block")),
        P(("group", "block"), None),
        P(("group", "block"), None),
    )
    return jax.shard_map(
        functools.partial(on_device, mesh.shape["group"], mesh.shape["block"]),
        mesh=mesh,
        in_specs=placed,
        out_specs=(P(("group", "block"), None), P(("group", "block"), None)),
        check_vma=False,
    )
```

time: 753 us -> 70 us (0.09)
  blocking collectives: 396 us -> 0 us
  waiting for transfers between devices: 261 us -> 0 us
  Pallas kernels: 0 us -> 62.7 us
  matrix products: 37.2 us -> 0 us
  other arithmetic: 19.4 us -> 0 us
  starting transfers between devices: 16.1 us -> 0 us
  local copies, waits for them, and re-layouts: 17.6 us -> 6.48 us
    psum x3 -> x0, blocking collectives: 293 us -> none  [the longest x2 207 us: global_norm(): return lax.psum(jnp.sum(residual * scaled_res), ('group', 'block'))]
    all_to_all x2 -> x0, waiting for transfers between devices: 261 us -> none  [the longest x1 261 us: on_device(): lax.all_to_all(send_blocks, 'block', split_axis=0, concat_axis=0, tiled=T...]
    unnamed x3 -> x0, blocking collectives: 66.5 us -> none
    pallas_call x0 -> x1, Pallas kernels: none -> 62.7 us  [on_device(): pl.pallas_call(functools.partial(cg_kernel, groups, owners, count, rows,...]
    dot_general x9 -> x0, matrix products: 37.2 us -> none  [the longest x2 20.3 us: on_device(): jnp.einsum('src,sc->sr', got_blocks, inputs, preferred_element_type=jnp.f...]
    all_gather x2 -> x0, blocking collectives: 36.1 us -> none  [on_device(): panel_low = lax.all_gather(low_field, 'group', axis=0, tiled=True)]
    all_to_all x2 -> x0, starting transfers between devices: 16.1 us -> none  [the longest x1 8.59 us: on_device(): lax.all_to_all(send_groups, 'block', split_axis=0, concat_axis=0, tiled=T...]
    scatter x2 -> x0, local copies, waits for them, and re-layouts: 8.46 us -> none  [the longest x1 7.72 us: on_device(): send_blocks = jnp.zeros((owners * capacity, row_count, block_width), jnp....]
  transfers between devices with their start and end apart: 2 -> 0, of which waited for: 1 -> 0; matrix products, arithmetic and copies ran while one was open for 3% -> 0% of each run, Pallas kernels for 0% -> 0%
where the time goes in v1:
time: 70 us; the launch traced here: 69.8 us
  Pallas kernels  62.7 us (90%)
  local copies, waits for them, and re-layouts  6.48 us (9%)
    pallas_call x1, Pallas kernels, on_device(): pl.pallas_call(functools.partial(cg_kernel, groups, owners, count, rows,...  62.7 us
    unnamed x14, local copies, waits for them, and re-layouts  6.48 us

profile of v1, /device:TPU:1, one launch (start us, length us, event | category | flops | bytes accessed | tf_op | source)
XLA Modules:
  0.0 69.8 jit_solution(10033353698802560386)
XLA Ops:
  0.6 0.0 copy-start
  0.6 2.0 %copy-done = bf16[12,128,1152]{2,1,0:T(8,128)(2,1)S(1)} copy-done((bf16[12,128,1152]{2,1,0:T(8,128)(2,1)S(1)}, bf16[12,128,1152]{2,1,0:T(8,128)(2,1)}, u32[]{:S(2)}) %copy-start) | copy-done | bytes 3538968
  2.6 0.0 copy-start.1
  2.6 0.7 copy-done.1
  3.3 0.0 copy-start.2
  3.3 0.7 copy-done.2
  4.0 0.0 copy-start.3
  4.0 0.7 copy-done.3
  4.7 0.0 copy-start.4
  4.7 0.7 copy-done.4
  5.3 0.0 copy-start.5
  5.3 0.7 copy-done.5
  6.0 62.7 %shard_map.77 = (f32[1,576]{1,0:T(1,128)S(1)}, f32[1,576]{1,0:T(1,128)S(1)}) custom-call(bf16[1536,1152]{1,0:T(8,128)(2,1)S(1)} %bitcast.1, s32[12]{0:T(128)S(1)} %copy-done.3, s32[12]{0:T(128)S(1)} %copy-done.4, s32[12]{0:T(128)S(1)} %copy-done.5, f32[1,576]{1,0:T(1,128)S(1)} %copy-done.1, f32[1,576]{1,0:T(1,128)S(1)} %copy-done.2), custom_call_target="tpu_custom_call" | custom-call | tf_op jit(solution)/shard_map/pallas_call | solution.py:330
  68.7 0.6 copy.10
  69.2 0.6 copy.11
Async XLA Ops:
  0.6 2.0 %copy-start = (bf16[12,128,1152]{2,1,0:T(8,128)(2,1)S(1)}, bf16[12,128,1152]{2,1,0:T(8,128)(2,1)}, u32[]{:S(2)}) copy-start(bf16[12,128,1152]{2,1,0:T(8,128)(2,1)} %param.6) | copy-start | bytes 10616836
  2.6 0.7 copy-start.1
  3.3 0.7 copy-start.2
  4.0 0.7 copy-start.3
  4.7 0.7 copy-start.4
  5.3 0.7 copy-start.5

commit v2 on v1

--- a/solution.py
+++ b/solution.py
@@ -27,10 +27,11 @@
 
 def cg_kernel(
     groups, owners, count, rows, params,
-    jac_hbm, dest_ref, other_ref, live_ref, damp_ref, rhs_ref,
+    jac_hbm, dest_hbm, other_hbm, live_hbm, damp_hbm, rhs_hbm,
     sol_ref, res_ref,
-    jac, pack, unpack, snd, rcv, ctx, wide, row_snd, row_rcv,
-    jac_sem, snd_sem, rcv_sem, zsnd_sem, zrcv_sem,
+    jac, dest_ref, other_ref, live_ref, damp_ref, rhs_ref,
+    pack, unpack, snd, rcv, ctx, wide, row_snd, row_rcv,
+    jac_sem, in_sem, snd_sem, rcv_sem, zsnd_sem, zrcv_sem,
 ):
     me_g = lax.axis_index("group")
     me_b = lax.axis_index("block")
@@ -43,6 +44,20 @@
         part = pl.ds(k * rows, rows)
         return pltpu.make_async_copy(jac_hbm.at[part], jac.at[part], jac_sem.at[k])
 
+    small = [
+        pltpu.make_async_copy(source, target, in_sem.at[i])
+        for i, (source, target) in enumerate(
+            [
+                (dest_hbm, dest_ref),
+                (other_hbm, other_ref),
+                (live_hbm, live_ref),
+                (damp_hbm, damp_ref),
+                (rhs_hbm, rhs_ref),
+            ]
+        )
+    ]
+    for copy in small:
+        copy.start()
     for k in range(count):
         block_copy(k).start()
 
@@ -105,6 +120,9 @@
 
     def group_wait(part, sem, stage):
         pltpu.make_async_copy(part, part, sem.at[stage]).wait()
+
+    for copy in small:
+        copy.wait()
 
     sub = iota((kpad, LANES), 0)
     lane = iota((kpad, LANES), 1)
@@ -185,12 +203,6 @@
 
     wide_lane = iota((groups, padded), 1)
     wide_row = iota((groups, padded), 0)
-    pl.semaphore_wait(barrier, owners - 1 + groups - 1)
-    ctx[me_g] = jnp.zeros((2, padded), F32)
-    ctx[me_g, 0:1, 0:params] = damp_ref[...]
-    ctx[me_g, 1:2, 0:params] = rhs_ref[...]
-    group_send(0, lambda peer: ctx.at[me_g], ctx.at[me_g])
-
     sum_rows = []
     for k in range(count):
         block_copy(k).wait()
@@ -200,6 +212,11 @@
         sum_rows.append(jnp.sum(kept * kept, axis=0, keepdims=True))
     sum_rows += [jnp.zeros((1, width), F32)] * (kpad - count)
     squares = jnp.concatenate(sum_rows, axis=0)
+    pl.semaphore_wait(barrier, owners - 1 + groups - 1)
+    ctx[me_g] = jnp.zeros((2, padded), F32)
+    ctx[me_g, 0:1, 0:params] = damp_ref[...]
+    ctx[me_g, 1:2, 0:params] = rhs_ref[...]
+    group_send(0, lambda peer: ctx.at[me_g], ctx.at[me_g])
     others = jnp.where(sub < count, other_col, 0).astype(F32).astype(BF16)
     other_out = dot(to_slot[owners:], others)
     send_terms(
@@ -224,18 +241,43 @@
     select = select[:, :kpad].astype(BF16)
     select_t = select_t[:kpad, : 3 * owners].astype(BF16)
 
+    def own_row(panel):
+        return jnp.sum(jnp.where(wide_row == me_g, panel, 0.0), axis=0, keepdims=True)
+
+    def split_row(value):
+        spot = iota((1, LANES), 1)
+        high = value.astype(BF16).astype(F32)
+        middle = (value - high).astype(BF16).astype(F32)
+        low = value - high - middle
+        return (
+            jnp.where(spot == 0, high, 0.0)
+            + jnp.where(spot == 1, middle, 0.0)
+            + jnp.where(spot == 2, low, 0.0)
+        )
+
     def sum_over_groups(stage, got, scalar):
         panel = dot(select_t, got)[:groups]
-        if scalar is not None:
-            spot = (wide_row == 0) & (wide_lane == params)
-            panel = jnp.where(spot, jnp.broadcast_to(scalar, panel.shape), panel)
-        wide[stage, me_g] = panel
+        high = panel.astype(BF16).astype(F32)
+        low = own_row(panel - high)
+        parts = [low[:, c * LANES : (c + 1) * LANES] for c in range(tiles)]
+        parts.append(jnp.zeros((1, LANES), F32) if scalar is None else split_row(scalar))
+        parts.append(jnp.zeros((groups - tiles - 1, LANES), F32))
+        extra = jnp.concatenate(parts, axis=0)
+        head = high[:, : 3 * LANES]
+        tail = jnp.concatenate([high[:, 3 * LANES :], extra], axis=1)
+        wide[stage, me_g] = jnp.concatenate([head, tail], axis=0).astype(BF16)
         group_send(1 + stage, lambda peer: wide.at[stage, me_g], wide.at[stage, me_g])
         group_wait(wide.at[stage, pl.ds(0, groups - 1)], zrcv_sem, 1 + stage)
-        out = wide[stage, 0]
-        for g in range(1, groups):
-            out = out + wide[stage, g]
-        return jnp.where(wide_lane < params, out, 0.0), total(jnp.where(wide_lane < params, 0.0, out))
+        out = jnp.zeros((groups, padded), F32)
+        scalar_out = jnp.zeros((1, LANES), F32)
+        for g in range(groups):
+            part = wide[stage, g].astype(F32)
+            out = out + jnp.concatenate([part[:groups], part[groups:, : 2 * LANES]], axis=1)
+            extra = part[groups:, 2 * LANES :]
+            low = jnp.concatenate([extra[c : c + 1] for c in range(tiles)], axis=1)
+            out = out + jnp.where(wide_row == g, jnp.broadcast_to(low, out.shape), 0.0)
+            scalar_out = scalar_out + extra[tiles : tiles + 1]
+        return out, total(scalar_out)
 
     def send_panel(stage, panel, last):
         low = jnp.concatenate([panel, jnp.zeros((kpad - groups, padded), F32)], axis=0)
@@ -249,9 +291,6 @@
         home = jnp.concatenate([home, fill], axis=1)
         far = pltpu.roll(jnp.concatenate([far, fill], axis=1), params, 1)
         return (home + far).astype(BF16)
-
-    def own_row(panel):
-        return jnp.sum(jnp.where(wide_row == me_g, panel, 0.0), axis=0, keepdims=True)
 
     summed, unused = sum_over_groups(0, got, None)
     group_wait(ctx.at[pl.ds(0, groups - 1)], zrcv_sem, 0)
@@ -326,33 +365,38 @@
     params = width // 2
     padded = (params + LANES - 1) // LANES * LANES
     vmem = pl.BlockSpec(memory_space=pltpu.VMEM)
-    smem = pl.BlockSpec(memory_space=pltpu.SMEM)
     return pl.pallas_call(
         functools.partial(cg_kernel, groups, owners, count, rows, params),
         out_shape=(
             jax.ShapeDtypeStruct(right_side.shape, F32),
             jax.ShapeDtypeStruct(right_side.shape, F32),
         ),
-        in_specs=[pl.BlockSpec(memory_space=pl.ANY), smem, smem, smem, vmem, vmem],
+        in_specs=[pl.BlockSpec(memory_space=pltpu.HBM)] * 6,
         out_specs=(vmem, vmem),
         scratch_shapes=[
             pltpu.VMEM((count * rows, width), BF16),
+            pltpu.SMEM((count,), jnp.int32),
+            pltpu.SMEM((count,), jnp.int32),
+            pltpu.SMEM((count,), jnp.int32),
+            pltpu.VMEM((1, params), F32),
+            pltpu.VMEM((1, params), F32),
             pltpu.VMEM((owners * MSG, LANES), F32),
             pltpu.VMEM((owners * MSG, LANES), F32),
             pltpu.VMEM((5, owners * MSG, LANES), BF16),
             pltpu.VMEM((5, owners * MSG, LANES), BF16),
             pltpu.VMEM((groups, 2, padded), F32),
-            pltpu.VMEM((2, groups, groups, padded), F32),
+            pltpu.VMEM((2, groups, 2 * groups, 3 * LANES), BF16),
             pltpu.VMEM((groups, 1, padded), F32),
             pltpu.VMEM((groups, 1, padded), F32),
             pltpu.SemaphoreType.DMA((count,)),
+            pltpu.SemaphoreType.DMA((5,)),
             pltpu.SemaphoreType.DMA((5,)),
             pltpu.SemaphoreType.DMA((5,)),
             pltpu.SemaphoreType.DMA((4,)),
             pltpu.SemaphoreType.DMA((4,)),
         ],
         compiler_params=pltpu.CompilerParams(
-            collective_id=0, has_side_effects=True, vmem_limit_bytes=40 * 1024 * 1024
+            collective_id=0, has_side_effects=True, vmem_limit_bytes=60 * 1024 * 1024
         ),
     )(
         jacobians.reshape(count * rows, width), destination, other_group, live_rows, damping, right_side

time: 70 us -> 61.5 us (0.88)
  Pallas kernels: 62.7 us -> 58.2 us
  local copies, waits for them, and re-layouts: 6.48 us -> 2.49 us
    pallas_call x1, Pallas kernels: 62.7 us -> 58.2 us  [on_device(): pl.pallas_call(functools.partial(cg_kernel, groups, owners, count, rows,...]
    unnamed x14 -> x2, local copies, waits for them, and re-layouts: 6.48 us -> 2.49 us
where the time goes in v2:
time: 61.5 us; the launch traced here: 61.3 us
  Pallas kernels  58.2 us (95%)
  local copies, waits for them, and re-layouts  2.49 us (4%)
  between operations  0.64 us (1%)
    pallas_call x1, Pallas kernels, on_device(): pl.pallas_call(functools.partial(cg_kernel, groups, owners, count, rows,...  58.2 us
    unnamed x2, local copies, waits for them, and re-layouts  2.49 us

profile of v2, /device:TPU:1, one launch (start us, length us, event | category | flops | bytes accessed | tf_op | source)
XLA Modules:
  0.0 61.3 jit_solution(5839740614027715862)
XLA Ops:
  0.6 58.2 %shard_map.77 = (f32[1,576]{1,0:T(1,128)}, f32[1,576]{1,0:T(1,128)}) custom-call(bf16[1536,1152]{1,0:T(8,128)(2,1)} %bitcast.1, s32[12]{0:T(128)} %dest_hbm.1, s32[12]{0:T(128)} %other_hbm.1, s32[12]{0:T(128)} %live_hbm.1, f32[1,576]{1,0:T(1,128)} %damp_hbm.1, f32[1,576]{1,0:T(1,128)} %rhs_hbm.1), custom_call_target="tpu_custom_call" | custom-call | tf_op jit(solution)/shard_map/pallas_call | solution.py:368
  58.8 1.3 %copy.10 = f32[1,576]{1,0:T(1,128)} copy(f32[1,576]{1,0:T(1,128)} %get-tuple-element.4) | data formatting | bytes 4608
  60.1 1.2 %copy.11 = f32[1,576]{1,0:T(1,128)} copy(f32[1,576]{1,0:T(1,128)} %get-tuple-element.5) | data formatting | bytes 4608

commit v3 on v2

--- a/solution.py
+++ b/solution.py
@@ -1,4 +1,5 @@
 import functools
+import itertools
 
 import jax
 import jax.numpy as jnp
@@ -25,10 +26,33 @@
     return lax.dot_general(left, right, (contract, ((), ())), preferred_element_type=F32)
 
 
+def block_dims(owners):
+    return (4, 4, 2) if owners == 32 else (1, owners // 2, 2)
+
+
+def distance(offset, dims):
+    return sum(min(step, size - step) for step, size in zip(offset[:2], dims))
+
+
+def peer_offsets(dims):
+    offsets = list(itertools.product(*[range(size) for size in dims]))
+    return sorted(offsets, key=lambda offset: (-distance(offset, dims), -offset[2]))
+
+
+def opposite(offset, dims):
+    return tuple((size - step) % size for step, size in zip(offset, dims))
+
+
+def peer_at(me, offset, dims):
+    x, y, core = me // (dims[1] * dims[2]), (me // dims[2]) % dims[1], me % dims[2]
+    x, y, core = ((at + step) % size for at, step, size in zip((x, y, core), offset, dims))
+    return (x * dims[1] + y) * dims[2] + core
+
+
 def cg_kernel(
     groups, owners, count, rows, params,
     jac_hbm, dest_hbm, other_hbm, live_hbm, damp_hbm, rhs_hbm,
-    sol_ref, res_ref,
+    out_ref,
     jac, dest_ref, other_ref, live_ref, damp_ref, rhs_ref,
     pack, unpack, snd, rcv, ctx, wide, row_snd, row_rcv,
     jac_sem, in_sem, snd_sem, rcv_sem, zsnd_sem, zrcv_sem,
@@ -39,6 +63,24 @@
     tiles = (params + LANES - 1) // LANES
     padded = tiles * LANES
     kpad = 16
+
+    dims = block_dims(owners)
+    offsets = peer_offsets(dims)
+    peers = [peer_at(me_b, offset, dims) for offset in offsets]
+    group_order = sorted(range(1, groups), key=lambda step: -min(step, groups - step))
+
+    barrier = pltpu.get_barrier_semaphore()
+    for peer in peers[:-1]:
+        pl.semaphore_signal(
+            barrier, inc=1, device_id=(me_g, peer), device_id_type=pl.DeviceIdType.MESH
+        )
+    for step in group_order:
+        pl.semaphore_signal(
+            barrier,
+            inc=1,
+            device_id=((me_g + step) % groups, me_b),
+            device_id_type=pl.DeviceIdType.MESH,
+        )
 
     def block_copy(k):
         part = pl.ds(k * rows, rows)
@@ -61,50 +103,28 @@
     for k in range(count):
         block_copy(k).start()
 
-    barrier = pltpu.get_barrier_semaphore()
-
-    def greet_block(step, carry):
-        peer = (me_b + step) % owners
-        pl.semaphore_signal(
-            barrier, inc=1, device_id=(me_g, peer), device_id_type=pl.DeviceIdType.MESH
-        )
-        return carry
-
-    def greet_group(step, carry):
-        peer = (me_g + step) % groups
-        pl.semaphore_signal(
-            barrier, inc=1, device_id=(peer, me_b), device_id_type=pl.DeviceIdType.MESH
-        )
-        return carry
-
-    lax.fori_loop(1, owners, greet_block, 0)
-    lax.fori_loop(1, groups, greet_group, 0)
-
-    def own_part():
-        return pl.ds(pl.multiple_of(me_b * MSG, MSG), MSG)
+    def slot_part(slot):
+        return pl.ds(slot * MSG, MSG)
 
     def block_send(stage):
-        def body(step, carry):
-            peer = (me_b + step) % owners
+        for slot, peer in enumerate(peers[:-1]):
+            there = offsets.index(opposite(offsets[slot], dims))
             pltpu.make_async_remote_copy(
-                src_ref=snd.at[stage, pl.ds(pl.multiple_of(peer * MSG, MSG), MSG)],
-                dst_ref=rcv.at[stage, own_part()],
+                src_ref=snd.at[stage, slot_part(slot)],
+                dst_ref=rcv.at[stage, slot_part(there)],
                 send_sem=snd_sem.at[stage],
                 recv_sem=rcv_sem.at[stage],
                 device_id=(me_g, peer),
                 device_id_type=pl.DeviceIdType.MESH,
             ).start()
-            return carry
-
-        lax.fori_loop(1, owners, body, 0)
-        rcv[stage, own_part()] = snd[stage, own_part()]
+        rcv[stage, slot_part(owners - 1)] = snd[stage, slot_part(owners - 1)]
 
     def block_wait(ref, sem, stage):
         part = ref.at[stage, pl.ds(0, (owners - 1) * MSG)]
         pltpu.make_async_copy(part, part, sem.at[stage]).wait()
 
     def group_send(stage, src_of, dst):
-        def body(step, carry):
+        for step in group_order:
             peer = (me_g + step) % groups
             pltpu.make_async_remote_copy(
                 src_ref=src_of(peer),
@@ -114,9 +134,6 @@
                 device_id=(peer, me_b),
                 device_id_type=pl.DeviceIdType.MESH,
             ).start()
-            return carry
-
-        lax.fori_loop(1, groups, body, 0)
 
     def group_wait(part, sem, stage):
         pltpu.make_async_copy(part, part, sem.at[stage]).wait()
@@ -141,12 +158,18 @@
     slot = iota((3 * owners, LANES), 0)
     dest_rows = jnp.broadcast_to(dest_row[:1], (3 * owners, LANES))
     rank_rows = jnp.broadcast_to(rank_row, (3 * owners, LANES))
-    slot_hit = dest_rows == slot % owners
+    slot_peer = iota((owners, LANES), 0)
+    for number, peer in enumerate(peers):
+        slot_peer = jnp.where(iota((owners, LANES), 0) == number, peer, slot_peer)
+    slot_hit = dest_rows == jnp.concatenate([slot_peer] * 3, axis=0)
     slot_rank = (slot // owners - 1).astype(F32)
     to_slot = jnp.where(slot_hit & ((slot < owners) | (rank_rows == slot_rank)), 1.0, 0.0)
     to_slot = to_slot[:, :kpad].astype(BF16)
     slot_lane = iota((kpad, LANES), 1)
-    lane_hit = dest_col == slot_lane % owners
+    lane_peer = jnp.zeros((kpad, LANES), jnp.int32)
+    for number, peer in enumerate(peers):
+        lane_peer = jnp.where(slot_lane % owners == number, peer, lane_peer)
+    lane_hit = dest_col == lane_peer
     lane_rank = (slot_lane // owners - 1).astype(F32)
     rank_cols = jnp.broadcast_to(rank_col, (kpad, LANES))
     from_home = jnp.where(lane_hit & (slot_lane < owners), 1.0, 0.0).astype(BF16)
@@ -349,8 +372,8 @@
     curvature = total(jnp.where(one_lane == params, out, 0.0))
     next_step = next_norm / curvature
     image = own_damping * next_direction + out
-    sol_ref[...] = (step_size * first_direction + next_step * next_direction)[:, :params]
-    res_ref[...] = (own_row(residual) - next_step * image)[:, :params]
+    out_ref[0:1] = (step_size * first_direction + next_step * next_direction)[:, :params]
+    out_ref[1:2] = (own_row(residual) - next_step * image)[:, :params]
 
     for stage in range(5):
         block_wait(snd, snd_sem, stage)
@@ -365,14 +388,13 @@
     params = width // 2
     padded = (params + LANES - 1) // LANES * LANES
     vmem = pl.BlockSpec(memory_space=pltpu.VMEM)
-    return pl.pallas_call(
+    out = pl.pallas_call(
         functools.partial(cg_kernel, groups, owners, count, rows, params),
         out_shape=(
-            jax.ShapeDtypeStruct(right_side.shape, F32),
-            jax.ShapeDtypeStruct(right_side.shape, F32),
+            jax.ShapeDtypeStruct((2, params), F32),
         ),
         in_specs=[pl.BlockSpec(memory_space=pltpu.HBM)] * 6,
-        out_specs=(vmem, vmem),
+        out_specs=(vmem,),
         scratch_shapes=[
             pltpu.VMEM((count * rows, width), BF16),
             pltpu.SMEM((count,), jnp.int32),
@@ -400,7 +422,8 @@
         ),
     )(
         jacobians.reshape(count * rows, width), destination, other_group, live_rows, damping, right_side
-    )
+    )[0]
+    return out[0:1], out[1:2]
 
 
 def solution(mesh):

time: 61.5 us -> 57.5 us (0.935)
  Pallas kernels: 58.2 us -> 55.3 us
  local copies, waits for them, and re-layouts: 2.49 us -> 1.35 us
    pallas_call x1, Pallas kernels: 58.2 us -> 55.3 us  [on_device(): pl.pallas_call(functools.partial(cg_kernel, groups, owners, count, rows,...]
    unnamed x2 -> x0, local copies, waits for them, and re-layouts: 2.49 us -> none
    slice x0 -> x1, local copies, waits for them, and re-layouts: none -> 1.35 us  [on_device(): return (out[0:1], out[1:2])]
where the time goes in v3:
time: 57.5 us; the launch traced here: 57.3 us
  Pallas kernels  55.3 us (96%)
  local copies, waits for them, and re-layouts  1.35 us (2%)
  between operations  0.64 us (1%)
    pallas_call x1, Pallas kernels, on_device(): pl.pallas_call(functools.partial(cg_kernel, groups, owners, count, rows,...  55.3 us
    slice x1, local copies, waits for them, and re-layouts, on_device(): return (out[0:1], out[1:2])  1.35 us

profile of v3, /device:TPU:1, one launch (start us, length us, event | category | flops | bytes accessed | tf_op | source)
XLA Modules:
  0.0 57.3 jit_solution(3403344304700001641)
XLA Ops:
  0.6 55.3 %shard_map.77 = f32[2,576]{1,0:T(2,128)} custom-call(bf16[1536,1152]{1,0:T(8,128)(2,1)} %bitcast.1, s32[12]{0:T(128)} %dest_hbm.1, s32[12]{0:T(128)} %other_hbm.1, s32[12]{0:T(128)} %live_hbm.1, f32[1,576]{1,0:T(1,128)} %damp_hbm.1, f32[1,576]{1,0:T(1,128)} %rhs_hbm.1), custom_call_target="tpu_custom_call" | custom-call | tf_op jit(solution)/shard_map/pallas_call | solution.py:391
  56.0 1.4 %fusion = (f32[1,576]{1,0:T(1,128)}, f32[1,576]{1,0:T(1,128)}) fusion(f32[2,576]{1,0:T(2,128)} %shard_map.77), kind=kLoop, calls=%fused_computation | loop fusion | bytes 9216 | tf_op jit(solution)/shard_map/slice | solution.py:426

commit v4 on v3

v4 whole, which is shorter than its diff:
```python
import functools
import itertools

import jax
import jax.numpy as jnp
from jax import lax
from jax.experimental import pallas as pl
from jax.experimental.pallas import tpu as pltpu
from jax.sharding import PartitionSpec as P

LANES = 128
MSG = 16
TERMS = 256
PANEL = 96
F32 = jnp.float32
BF16 = jnp.bfloat16


def total(value):
    return jnp.sum(jnp.sum(value, axis=1, keepdims=True), axis=0, keepdims=True)


def iota(shape, dim):
    return lax.broadcasted_iota(jnp.int32, shape, dim)


def dot(left, right, contract=((1,), (0,))):
    return lax.dot_general(left, right, (contract, ((), ())), preferred_element_type=F32)


def block_dims(owners):
    return (4, 4, 2) if owners == 32 else (1, owners // 2, 2)


def distance(offset, dims):
    return sum(min(step, size - step) for step, size in zip(offset[:2], dims))


def peer_offsets(dims):
    offsets = list(itertools.product(*[range(size) for size in dims]))
    return sorted(offsets, key=lambda offset: (-distance(offset, dims), -offset[2]))


def opposite(offset, dims):
    return tuple((size - step) % size for step, size in zip(offset, dims))


def peer_at(me, offset, dims):
    x, y, core = me // (dims[1] * dims[2]), (me // dims[2]) % dims[1], me % dims[2]
    x, y, core = ((at + step) % size for at, step, size in zip((x, y, core), offset, dims))
    return (x * dims[1] + y) * dims[2] + core


def scalar_row(last, total_rows):
    spot = (iota((16, total_rows), 1) & (MSG - 1)) == last
    return jnp.where(spot & (iota((16, total_rows), 0) == 0), 1.0, 0.0).astype(BF16)


def cg_kernel(
    groups, owners, count, rows, params,
    jac_hbm, dest_hbm, other_hbm, live_hbm, damp_hbm, rhs_hbm,
    out_ref,
    jac, jac_t, dest_ref, other_ref, live_ref, damp_ref, rhs_ref,
    unpack, extras, term_map, input_map, panel_map, row_map, snd, rcv, ctx, wide, row_snd, row_rcv,
    jac_sem, in_sem, snd_sem, rcv_sem, zsnd_sem, zrcv_sem,
):
    me_g = lax.axis_index("group")
    me_b = lax.axis_index("block")
    width = jac.shape[1]
    tiles = (params + LANES - 1) // LANES
    padded = tiles * LANES
    kpad = 16
    raw = width // LANES
    total_rows = owners * MSG
    late = min(8, owners // 2)
    chunks = sorted({(0, late), (late, 2 * late), (2 * late, owners)} - {(owners, owners)})

    dims = block_dims(owners)
    offsets = peer_offsets(dims)
    peers = [peer_at(me_b, offset, dims) for offset in offsets]
    group_order = sorted(range(1, groups), key=lambda step: -min(step, groups - step))

    barrier = pltpu.get_barrier_semaphore()
    for step in group_order:
        pl.semaphore_signal(
            barrier,
            inc=1,
            device_id=((me_g + step) % groups, me_b),
            device_id_type=pl.DeviceIdType.MESH,
        )
    for peer in peers[:-1]:
        pl.semaphore_signal(
            barrier, inc=1, device_id=(me_g, peer), device_id_type=pl.DeviceIdType.MESH
        )

    def block_copy(k):
        part = pl.ds(k * rows, rows)
        return pltpu.make_async_copy(jac_hbm.at[part], jac.at[part], jac_sem.at[k])

    small = [
        pltpu.make_async_copy(source, target, in_sem.at[i])
        for i, (source, target) in enumerate(
            [
                (dest_hbm, dest_ref),
                (other_hbm, other_ref),
                (live_hbm, live_ref),
                (damp_hbm, damp_ref),
                (rhs_hbm, rhs_ref),
            ]
        )
    ]
    for copy in small:
        copy.start()
    for k in range(count):
        block_copy(k).start()

    def slot_part(slot):
        return pl.ds(slot * MSG, MSG)

    def block_send(stage, first, end):
        for slot in range(first, min(end, owners - 1)):
            there = offsets.index(opposite(offsets[slot], dims))
            pltpu.make_async_remote_copy(
                src_ref=snd.at[stage, slot_part(slot)],
                dst_ref=rcv.at[stage, slot_part(there)],
                send_sem=snd_sem.at[stage],
                recv_sem=rcv_sem.at[stage, 0 if there < late else 1],
                device_id=(me_g, peers[slot]),
                device_id_type=pl.DeviceIdType.MESH,
            ).start()

    def block_wait_near(stage):
        part = rcv.at[stage, pl.ds(late * MSG, (owners - 1 - late) * MSG)]
        pltpu.make_async_copy(part, part, rcv_sem.at[stage, 1]).wait()

    def block_wait_far(stage):
        part = rcv.at[stage, pl.ds(0, late * MSG)]
        pltpu.make_async_copy(part, part, rcv_sem.at[stage, 0]).wait()

    def block_wait_sent(stage):
        part = snd.at[stage, pl.ds(0, (owners - 1) * MSG)]
        pltpu.make_async_copy(part, part, snd_sem.at[stage]).wait()

    def group_send(stage, src_of, dst):
        for step in group_order:
            peer = (me_g + step) % groups
            pltpu.make_async_remote_copy(
                src_ref=src_of(peer),
                dst_ref=dst,
                send_sem=zsnd_sem.at[stage],
                recv_sem=zrcv_sem.at[stage],
                device_id=(peer, me_b),
                device_id_type=pl.DeviceIdType.MESH,
            ).start()

    def group_wait(part, sem, stage):
        pltpu.make_async_copy(part, part, sem.at[stage]).wait()

    for copy in small:
        copy.wait()

    half = params // LANES
    near = groups * tiles
    sub = iota((kpad, TERMS), 0)
    lane = iota((kpad, TERMS), 1)
    block_lane = lane & (kpad - 1)
    dest_col = jnp.full((kpad, TERMS), -1, jnp.int32)
    dest_row = jnp.full((kpad, TERMS), -1, jnp.int32)
    live_col = jnp.zeros((kpad, LANES), jnp.int32)
    other_col = jnp.zeros((kpad, LANES), jnp.int32)
    for k in range(count):
        dest_col = jnp.where(sub == k, dest_ref[k], dest_col)
        dest_row = jnp.where(block_lane == k, dest_ref[k], dest_row)
        live_col = jnp.where(sub[:, :LANES] == k, live_ref[k], live_col)
        other_col = jnp.where(sub[:, :LANES] == k, other_ref[k], other_col)
    same = jnp.where((dest_col == dest_row) & (dest_row >= 0), 1.0, 0.0)
    rank_row = jnp.sum(jnp.where(sub < block_lane, same, 0.0), axis=0, keepdims=True)
    rank_col = jnp.sum(jnp.where((lane < sub), same, 0.0), axis=1, keepdims=True)
    slot_peer = jnp.zeros((owners, TERMS), jnp.int32)
    for number, peer in enumerate(peers):
        slot_peer = jnp.where(iota((owners, TERMS), 0) == number, peer, slot_peer)
    hit = jnp.where(jnp.broadcast_to(dest_row[:1], (owners, TERMS)) == slot_peer, 1.0, 0.0)
    rank = jnp.broadcast_to(rank_row, (owners, TERMS))
    to_slot = jnp.concatenate(
        [hit, jnp.where(rank == 0.0, hit, 0.0), jnp.where(rank == 1.0, hit, 0.0)], axis=0
    ).astype(BF16)

    def segment(row):
        return jnp.where(row < tiles, 0, jnp.where(row < 2 * tiles, 1, jnp.where(row < 3 * tiles, 2, 0)))

    row_at = iota((total_rows, 3 * owners), 0)
    slot_at = iota((total_rows, 3 * owners), 1)
    spread = (
        jnp.where(
            (row_at >> 4) + owners * segment(row_at & (MSG - 1)) == slot_at, 1.0, 0.0
        )
    ).astype(BF16)
    row = iota((total_rows, TERMS), 0) & (MSG - 1)
    term_lane = iota((total_rows, TERMS), 1)
    tile = term_lane >> 4
    last = 3 * tiles
    wanted = jnp.where(row < tiles, row, jnp.where(row < 2 * tiles, row - tiles, row - 2 * tiles) + half)
    allowed = (row < last) & ((tile == wanted) | ((row < tiles) & (tile == raw + row)))
    terms_to_rows = jnp.where(allowed, dot(spread, to_slot), 0.0)
    terms_to_rows = jnp.where((row == last) & (term_lane == kpad - 1), 1.0, terms_to_rows)
    term_map[...] = terms_to_rows.astype(BF16)
    input_map[...] = terms_to_rows.T[: raw * kpad].astype(BF16)
    keep = jnp.concatenate(
        [
            jnp.where((sub[:, :LANES] == k) & (lane[:, :LANES] < live_col), 1.0, 0.0)
            for k in range(count)
        ],
        axis=1,
    )
    def panel_target(row, ids_a, ids_b):
        part = segment(row)
        far = jnp.where(part == 1, row - tiles, row - 2 * tiles) * groups + near
        far = far.astype(F32) + jnp.where(part == 1, ids_a, ids_b)
        home = (row * groups + me_g).astype(F32)
        return jnp.where(row == last, float(2 * near), jnp.where(row < tiles, home, far))

    others = other_col.astype(F32).astype(BF16)
    ids = dot(to_slot[owners:, :kpad], others)
    there = jnp.zeros((owners, LANES), jnp.int32)
    for number, offset in enumerate(offsets):
        place = offsets.index(opposite(offset, dims))
        there = jnp.where(iota((owners, LANES), 0) == number, place, there)
    slot_lane = iota((owners, LANES), 1)
    targets = panel_target(slot_lane & (MSG - 1), ids[:owners], ids[owners:])
    per_tile = LANES // MSG
    unpack[...] = jnp.zeros((total_rows, LANES), F32)
    unpack[pl.ds(last, owners, stride=MSG), :] = jnp.where(
        (slot_lane >> 4) == (there & (per_tile - 1)), targets, 0.0
    )

    def tiles_of(value, first, number):
        return [value[:, c * LANES : (c + 1) * LANES] for c in range(first, first + number)]

    def send_rows(stage, row_of, values, extra=None):
        for first, end in chunks:
            part = pl.ds(first * MSG, (end - first) * MSG)
            out = dot(row_of[part], values)
            out = (out if extra is None else out + extra[part]).astype(BF16)
            snd[stage, part] = out
            block_send(stage, first, end)
        rcv[stage, slot_part(owners - 1)] = out[-MSG:]

    def receive_rows(stage, map_ref):
        block_wait_near(stage)
        near_rows = pl.ds(late * MSG, total_rows - late * MSG)
        out = dot(map_ref[:, late * MSG :], rcv[stage, near_rows])
        block_wait_far(stage)
        return out + dot(map_ref[:, : late * MSG], rcv[stage, pl.ds(0, late * MSG)])

    def send_terms(stage, terms, last_row, extra=None):
        high = terms.astype(BF16)
        low = (terms[:, :padded] - high[:, :padded].astype(F32)).astype(BF16)
        parts = tiles_of(high, 0, raw)
        if last_row is not None:
            carrier = jnp.where(sub[:, :LANES] == kpad - 1, last_row, terms[:, :LANES])
            parts[0] = carrier.astype(BF16)
        parts += tiles_of(low, 0, tiles)
        blank = jnp.zeros((kpad, LANES), BF16)
        parts += [blank] * (TERMS // kpad - len(parts))
        send_rows(stage, term_map, jnp.concatenate(parts, axis=0), extra)

    wide_lane = iota((groups, padded), 1)
    wide_row = iota((groups, padded), 0)
    valid = wide_lane < params
    shift = params % LANES

    def receive_terms(stage):
        if stage == 0:
            out = dot(panel_map[...], rcv[0])
        else:
            out = receive_rows(stage, panel_map)
        home = jnp.concatenate([out[c * groups : (c + 1) * groups] for c in range(tiles)], axis=1)
        far = jnp.concatenate(
            [out[near + c * groups : near + (c + 1) * groups] for c in range(tiles)], axis=1
        )
        panel = home + pltpu.roll(far, padded - shift, 1)
        return jnp.where(valid, panel, 0.0), out[2 * near : 2 * near + 1]

    def send_panel(stage, panel, last_row):
        parts = tiles_of(panel, 0, tiles) + tiles_of(pltpu.roll(panel, shift, 1), 0, tiles)
        parts.append(jnp.broadcast_to(last_row, (groups, LANES)))
        parts.append(jnp.zeros((PANEL - 2 * near - groups, LANES), F32))
        send_rows(stage, row_map, jnp.concatenate(parts, axis=0).astype(BF16))

    def receive_inputs(stage):
        out = receive_rows(stage, input_map)
        inputs = jnp.concatenate([out[t * kpad : (t + 1) * kpad] for t in range(raw)], axis=1)
        return inputs.astype(BF16)

    one = iota((1, LANES), 1)

    def split(value, first):
        high = value.astype(BF16).astype(F32)
        middle = (value - high).astype(BF16).astype(F32)
        low = value - high - middle
        out = jnp.where(one == first, high, 0.0) + jnp.where(one == first + 1, middle, 0.0)
        return out + jnp.where(one == first + 2, low, 0.0)

    def lanes_of(value):
        value = jnp.sum(value, axis=0, keepdims=True)
        folded = sum(tiles_of(value, 0, tiles)[1:], value[:, :LANES])
        folded = folded + pltpu.roll(folded, LANES // 2, 1)
        high = folded.astype(BF16).astype(F32)
        return jnp.where(one < LANES // 2, high, folded - high)

    def own_row(panel):
        return jnp.sum(jnp.where(wide_row == me_g, panel, 0.0), axis=0, keepdims=True)

    def sum_over_groups(stage, panel, scalar):
        high = panel.astype(BF16).astype(F32)
        low = own_row(panel - high)
        parts = tiles_of(low, 0, tiles)
        scalar = jnp.zeros((1, LANES), F32) if scalar is None else scalar
        first = scalar.astype(BF16).astype(F32)
        second = (scalar - first).astype(BF16).astype(F32)
        parts += [first, second, scalar - first - second]
        extra = jnp.concatenate(parts, axis=0)
        head = high[:, : 3 * LANES]
        tail = jnp.concatenate([high[:, 3 * LANES :], extra], axis=1)
        wide[stage, me_g] = jnp.concatenate([head, tail], axis=0).astype(BF16)
        group_send(1 + stage, lambda peer: wide.at[stage, me_g], wide.at[stage, me_g])

    def summed_groups(stage):
        group_wait(wide.at[stage, pl.ds(0, groups - 1)], zrcv_sem, 1 + stage)
        out = jnp.zeros((groups, padded), F32)
        for g in range(groups):
            part = wide[stage, g].astype(F32)
            out = out + jnp.concatenate([part[:groups], part[groups:, : 2 * LANES]], axis=1)
            extras[stage, g * groups : (g + 1) * groups] = part[groups:, 2 * LANES :]
        rest = [extras[stage, pl.ds(c, groups, stride=groups), :] for c in range(groups)]
        scalar = total(rest[tiles] + rest[tiles + 1] + rest[tiles + 2])
        return out + jnp.concatenate(rest[:tiles], axis=1), scalar

    sum_rows = []
    for k in range(count):
        block_copy(k).wait()
        block = jac[k * rows : (k + 1) * rows, :].astype(F32)
        live = iota((rows, width), 0) < live_ref[k]
        kept = jnp.where(live, block, 0.0)
        sum_rows.append(jnp.sum(kept * kept, axis=0, keepdims=True))
        jac_t[:, k * rows : (k + 1) * rows] = jac[k * rows : (k + 1) * rows, :].T
    sum_rows += [jnp.zeros((1, width), F32)] * (kpad - count)
    squares = jnp.concatenate(sum_rows, axis=0)

    ctx[me_g] = jnp.zeros((2, padded), F32)
    ctx[me_g, 0:1, 0:params] = damp_ref[...]
    ctx[me_g, 1:2, 0:params] = rhs_ref[...]
    pl.semaphore_wait(barrier, owners - 1 + groups - 1)
    send_terms(0, squares, None, unpack)
    group_send(0, lambda peer: ctx.at[me_g], ctx.at[me_g])
    block_wait_near(0)
    block_wait_far(0)
    decode_lane = iota((kpad, total_rows), 1)
    decode = jnp.where(
        ((decode_lane & (MSG - 1)) == last)
        & ((decode_lane >> 4) // per_tile == iota((kpad, total_rows), 0)),
        1.0,
        0.0,
    ).astype(BF16)
    decoded = dot(decode, rcv[0])
    target = jnp.concatenate(
        [
            jnp.broadcast_to(decoded[t : t + 1], (groups, LANES))
            for t in range((total_rows + LANES - 1) // LANES)
        ],
        axis=1,
    )[:, :total_rows]
    panel_row = iota((groups, total_rows), 0).astype(F32)
    rows_to_panel = jnp.concatenate(
        [
            jnp.where(target == panel_row + float(first), 1.0, 0.0)
            for first in range(0, LANES, groups)
        ],
        axis=0,
    )
    panel_map[...] = rows_to_panel[:PANEL].astype(BF16)
    panel, unused = receive_terms(0)
    sum_over_groups(0, panel, None)
    row_map[...] = rows_to_panel.T[:, :PANEL].astype(BF16)
    group_wait(ctx.at[pl.ds(0, groups - 1)], zrcv_sem, 0)
    damping = jnp.concatenate([ctx[g, 0:1, :] for g in range(groups)], axis=0)
    right_side = jnp.concatenate([ctx[g, 1:2, :] for g in range(groups)], axis=0)
    summed, unused = summed_groups(0)
    diagonal = jnp.where(valid, damping + summed, 1.0)
    direction = right_side / diagonal

    send_panel(1, direction, lanes_of(right_side * direction))
    first_direction = own_row(direction)
    own_damping = own_row(damping)
    damped_direction = damping * direction
    damped = total(own_damping * first_direction * first_direction)
    inputs = receive_inputs(1)
    product = dot(inputs, jac_t[...])
    kept = product * keep
    projected = kept.astype(BF16)
    returned = dot(projected, jac[...])
    send_terms(2, returned, split(damped + total(kept * projected.astype(F32)), 0))
    scalars = dot(scalar_row(last, total_rows), rcv[1])[:1]
    norm = total(scalars)
    panel, scalars = receive_terms(2)
    sum_over_groups(1, panel, scalars)
    summed, curvature = summed_groups(1)
    step_size = norm / curvature
    residual = right_side - step_size * (damped_direction + summed)
    scaled = residual / diagonal

    send_panel(3, scaled, lanes_of(residual * scaled))
    own_scaled = own_row(scaled)
    own_residual = own_row(residual)
    inputs = receive_inputs(3)
    next_norm = total(dot(scalar_row(last, total_rows), rcv[3])[:1])
    beta = next_norm / norm
    product = dot(inputs, jac_t[...]) + beta * product
    kept = product * keep
    projected = kept.astype(BF16)
    returned = dot(projected, jac[...])
    next_direction = own_scaled + beta * first_direction
    partial = total(kept * projected.astype(F32)) + total(
        own_damping * next_direction * next_direction
    )
    send_terms(4, returned, split(partial, 0))
    panel, scalars = receive_terms(4)
    panel = jnp.where(wide_lane == params, jnp.broadcast_to(total(scalars), panel.shape), panel)
    for g in range(groups):
        row_snd[g] = panel[g : g + 1]
    row_rcv[me_g] = own_row(panel)
    group_send(3, lambda peer: row_snd.at[peer], row_rcv.at[me_g])
    group_wait(row_rcv.at[pl.ds(0, groups - 1)], zrcv_sem, 3)
    out = row_rcv[0]
    for g in range(1, groups):
        out = out + row_rcv[g]
    one_lane = iota((1, padded), 1)
    curvature = total(jnp.where(one_lane == params, out, 0.0))
    next_step = next_norm / curvature
    image = own_damping * next_direction + out
    out_ref[0:1] = (step_size * first_direction + next_step * next_direction)[:, :params]
    out_ref[1:2] = (own_residual - next_step * image)[:, :params]

    for stage in range(5):
        block_wait_sent(stage)
    group_wait(ctx.at[pl.ds(0, groups - 1)], zsnd_sem, 0)
    for stage in range(2):
        group_wait(wide.at[stage, pl.ds(0, groups - 1)], zsnd_sem, 1 + stage)
    group_wait(row_snd.at[pl.ds(0, groups - 1)], zsnd_sem, 3)


def on_device(groups, owners, jacobians, destination, other_group, live_rows, damping, right_side):
    count, rows, width = jacobians.shape
    params = width // 2
    padded = (params + LANES - 1) // LANES * LANES
    vmem = pl.BlockSpec(memory_space=pltpu.VMEM)
    flat = jacobians.reshape(count * rows, width)
    operands = [flat, destination, other_group, live_rows, damping, right_side]
    out = pl.pallas_call(
        functools.partial(cg_kernel, groups, owners, count, rows, params),
        out_shape=(
            jax.ShapeDtypeStruct((2, params), F32),
        ),
        in_specs=[pl.BlockSpec(memory_space=pltpu.HBM)] * 6,
        out_specs=(vmem,),
        scratch_shapes=[
            pltpu.VMEM((count * rows, width), BF16),
            pltpu.VMEM((width, count * rows), BF16),
            pltpu.SMEM((count,), jnp.int32),
            pltpu.SMEM((count,), jnp.int32),
            pltpu.SMEM((count,), jnp.int32),
            pltpu.VMEM((1, params), F32),
            pltpu.VMEM((1, params), F32),
            pltpu.VMEM((owners * MSG, LANES), F32),
            pltpu.VMEM((2, groups * groups, LANES), F32),
            pltpu.VMEM((owners * MSG, TERMS), BF16),
            pltpu.VMEM((width // LANES * 16, owners * MSG), BF16),
            pltpu.VMEM((PANEL, owners * MSG), BF16),
            pltpu.VMEM((owners * MSG, PANEL), BF16),
            pltpu.VMEM((5, owners * MSG, LANES), BF16),
            pltpu.VMEM((5, owners * MSG, LANES), BF16),
            pltpu.VMEM((groups, 2, padded), F32),
            pltpu.VMEM((2, groups, 2 * groups, 3 * LANES), BF16),
            pltpu.VMEM((groups, 1, padded), F32),
            pltpu.VMEM((groups, 1, padded), F32),
            pltpu.SemaphoreType.DMA((count,)),
            pltpu.SemaphoreType.DMA((5,)),
            pltpu.SemaphoreType.DMA((5,)),
            pltpu.SemaphoreType.DMA((5, 2)),
            pltpu.SemaphoreType.DMA((4,)),
            pltpu.SemaphoreType.DMA((4,)),
        ],
        compiler_params=pltpu.CompilerParams(
            collective_id=0, has_side_effects=True, vmem_limit_bytes=40 * 1024 * 1024
        ),
    )(
        *[pltpu.with_memory_space_constraint(operand, pltpu.HBM) for operand in operands]
    )[0]
    return out[0:1], out[1:2]


def solution(mesh):
    placed = (
        P(("group", "block"), None, None),
        P(("group", "block")),
        P(("group", "block")),
        P(("group", "block")),
        P(("group", "block"), None),
        P(("group", "block"), None),
    )
    return jax.shard_map(
        functools.partial(on_device, mesh.shape["group"], mesh.shape["block"]),
        mesh=mesh,
        in_specs=placed,
        out_specs=(P(("group", "block"), None), P(("group", "block"), None)),
        check_vma=False,
    )
```

time: 57.5 us -> 56.1 us (0.976)
  local copies, waits for them, and re-layouts: 1.35 us -> 0.59 us
    slice x1, local copies, waits for them, and re-layouts: 1.35 us -> 0.59 us  [on_device(): return (out[0:1], out[1:2])]
    pallas_call x1, Pallas kernels: 55.3 us -> 54.8 us  [on_device(): pl.pallas_call(functools.partial(cg_kernel, groups, owners, count, rows,...]
where the time goes in v4:
time: 56.1 us; the launch traced here: 56 us
  Pallas kernels  54.8 us (98%)
  between operations  0.64 us (1%)
  local copies, waits for them, and re-layouts  0.59 us (1%)
    pallas_call x1, Pallas kernels, on_device(): pl.pallas_call(functools.partial(cg_kernel, groups, owners, count, rows,...  54.8 us

profile of v4, /device:TPU:1, one launch (start us, length us, event | category | flops | bytes accessed | tf_op | source)
XLA Modules:
  0.0 56.0 jit_solution(12654341500251197651)
XLA Ops:
  0.6 54.8 %shard_map.77 = f32[2,576]{1,0:T(2,128)S(1)} custom-call(bf16[1536,1152]{1,0:T(8,128)(2,1)} %bitcast.1, s32[12]{0:T(128)} %dest_hbm.1, s32[12]{0:T(128)} %other_hbm.1, s32[12]{0:T(128)} %live_hbm.1, f32[1,576]{1,0:T(1,128)} %damp_hbm.1, f32[1,576]{1,0:T(1,128)} %rhs_hbm.1), custom_call_target="tpu_custom_call" | custom-call | tf_op jit(solution)/shard_map/pallas_call | solution.py:459
  55.4 0.6 %fusion = (f32[1,576]{1,0:T(1,128)}, f32[1,576]{1,0:T(1,128)}) fusion(f32[2,576]{1,0:T(2,128)S(1)} %shard_map.77), kind=kLoop, calls=%fused_computation | loop fusion | bytes 9216 | tf_op jit(solution)/shard_map/slice | solution.py:499

commit v5 on v4

--- a/solution.py
+++ b/solution.py
@@ -270,10 +270,9 @@
     shift = params % LANES
 
     def receive_terms(stage):
-        if stage == 0:
-            out = dot(panel_map[...], rcv[0])
-        else:
-            out = receive_rows(stage, panel_map)
+        return panel_of(receive_rows(stage, panel_map))
+
+    def panel_of(out):
         home = jnp.concatenate([out[c * groups : (c + 1) * groups] for c in range(tiles)], axis=1)
         far = jnp.concatenate(
             [out[near + c * groups : near + (c + 1) * groups] for c in range(tiles)], axis=1
@@ -353,8 +352,6 @@
     pl.semaphore_wait(barrier, owners - 1 + groups - 1)
     send_terms(0, squares, None, unpack)
     group_send(0, lambda peer: ctx.at[me_g], ctx.at[me_g])
-    block_wait_near(0)
-    block_wait_far(0)
     decode_lane = iota((kpad, total_rows), 1)
     decode = jnp.where(
         ((decode_lane & (MSG - 1)) == last)
@@ -362,25 +359,36 @@
         1.0,
         0.0,
     ).astype(BF16)
-    decoded = dot(decode, rcv[0])
-    target = jnp.concatenate(
-        [
-            jnp.broadcast_to(decoded[t : t + 1], (groups, LANES))
-            for t in range((total_rows + LANES - 1) // LANES)
-        ],
-        axis=1,
-    )[:, :total_rows]
     panel_row = iota((groups, total_rows), 0).astype(F32)
-    rows_to_panel = jnp.concatenate(
-        [
-            jnp.where(target == panel_row + float(first), 1.0, 0.0)
-            for first in range(0, LANES, groups)
-        ],
-        axis=0,
-    )
-    panel_map[...] = rows_to_panel[:PANEL].astype(BF16)
-    panel, unused = receive_terms(0)
+
+    def decode_rows(first, end):
+        got = rcv[0, first:end]
+        decoded = dot(decode[:, first:end], got)
+        target = jnp.concatenate(
+            [
+                jnp.broadcast_to(decoded[t : t + 1], (groups, LANES))
+                for t in range((total_rows + LANES - 1) // LANES)
+            ],
+            axis=1,
+        )[:, first:end]
+        mapped = jnp.concatenate(
+            [
+                jnp.where(target == panel_row[:, first:end] + float(at), 1.0, 0.0)
+                for at in range(0, LANES, groups)
+            ],
+            axis=0,
+        )
+        low_map = mapped[:PANEL].astype(BF16)
+        panel_map[:, first:end] = low_map
+        return mapped, dot(low_map, got)
+
+    block_wait_near(0)
+    near_map, near_out = decode_rows(late * MSG, total_rows)
+    block_wait_far(0)
+    far_map, far_out = decode_rows(0, late * MSG)
+    panel, unused = panel_of(near_out + far_out)
     sum_over_groups(0, panel, None)
+    rows_to_panel = jnp.concatenate([far_map, near_map], axis=1)
     row_map[...] = rows_to_panel.T[:, :PANEL].astype(BF16)
     group_wait(ctx.at[pl.ds(0, groups - 1)], zrcv_sem, 0)
     damping = jnp.concatenate([ctx[g, 0:1, :] for g in range(groups)], axis=0)
@@ -424,29 +432,31 @@
         own_damping * next_direction * next_direction
     )
     send_terms(4, returned, split(partial, 0))
+    for stage in range(4):
+        block_wait_sent(stage)
+    group_wait(ctx.at[pl.ds(0, groups - 1)], zsnd_sem, 0)
+    for stage in range(2):
+        group_wait(wide.at[stage, pl.ds(0, groups - 1)], zsnd_sem, 1 + stage)
     panel, scalars = receive_terms(4)
-    panel = jnp.where(wide_lane == params, jnp.broadcast_to(total(scalars), panel.shape), panel)
+    spare = jnp.concatenate([scalars] * tiles, axis=1)
+    spare = pltpu.roll(spare, shift, 1)
+    panel = jnp.where(valid, panel, jnp.broadcast_to(spare, panel.shape))
     for g in range(groups):
         row_snd[g] = panel[g : g + 1]
     row_rcv[me_g] = own_row(panel)
     group_send(3, lambda peer: row_snd.at[peer], row_rcv.at[me_g])
+    block_wait_sent(4)
+    group_wait(row_snd.at[pl.ds(0, groups - 1)], zsnd_sem, 3)
     group_wait(row_rcv.at[pl.ds(0, groups - 1)], zrcv_sem, 3)
     out = row_rcv[0]
     for g in range(1, groups):
         out = out + row_rcv[g]
     one_lane = iota((1, padded), 1)
-    curvature = total(jnp.where(one_lane == params, out, 0.0))
+    curvature = total(jnp.where(one_lane < params, 0.0, out))
     next_step = next_norm / curvature
     image = own_damping * next_direction + out
     out_ref[0:1] = (step_size * first_direction + next_step * next_direction)[:, :params]
     out_ref[1:2] = (own_residual - next_step * image)[:, :params]
-
-    for stage in range(5):
-        block_wait_sent(stage)
-    group_wait(ctx.at[pl.ds(0, groups - 1)], zsnd_sem, 0)
-    for stage in range(2):
-        group_wait(wide.at[stage, pl.ds(0, groups - 1)], zsnd_sem, 1 + stage)
-    group_wait(row_snd.at[pl.ds(0, groups - 1)], zsnd_sem, 3)
 
 
 def on_device(groups, owners, jacobians, destination, other_group, live_rows, damping, right_side):

time: 56.1 us -> 56.2 us (level)
  no operation moved by 1% of the time
where the time goes in v5:
time: 56.2 us; the launch traced here: 56.1 us
  Pallas kernels  54.8 us (98%)
  between operations  0.64 us (1%)
  local copies, waits for them, and re-layouts  0.59 us (1%)
    pallas_call x1, Pallas kernels, on_device(): pl.pallas_call(functools.partial(cg_kernel, groups, owners, count, rows,...  54.8 us

profile of v5, /device:TPU:1, one launch (start us, length us, event | category | flops | bytes accessed | tf_op | source)
XLA Modules:
  0.0 56.1 jit_solution(11035532116138723786)
XLA Ops:
  0.6 54.8 %shard_map.77 = f32[2,576]{1,0:T(2,128)S(1)} custom-call(bf16[1536,1152]{1,0:T(8,128)(2,1)} %bitcast.1, s32[12]{0:T(128)} %dest_hbm.1, s32[12]{0:T(128)} %other_hbm.1, s32[12]{0:T(128)} %live_hbm.1, f32[1,576]{1,0:T(1,128)} %damp_hbm.1, f32[1,576]{1,0:T(1,128)} %rhs_hbm.1), custom_call_target="tpu_custom_call" | custom-call | tf_op jit(solution)/shard_map/pallas_call | solution.py:469
  55.5 0.6 %fusion = (f32[1,576]{1,0:T(1,128)}, f32[1,576]{1,0:T(1,128)}) fusion(f32[2,576]{1,0:T(2,128)S(1)} %shard_map.77), kind=kLoop, calls=%fused_computation | loop fusion | bytes 9216 | tf_op jit(solution)/shard_map/slice | solution.py:509

commit v6 on v5

--- a/solution.py
+++ b/solution.py
@@ -141,17 +141,20 @@
         part = snd.at[stage, pl.ds(0, (owners - 1) * MSG)]
         pltpu.make_async_copy(part, part, snd_sem.at[stage]).wait()
 
-    def group_send(stage, src_of, dst):
+    def group_send(stage, src_of, dst, far_sem=None):
         for step in group_order:
             peer = (me_g + step) % groups
             pltpu.make_async_remote_copy(
                 src_ref=src_of(peer),
                 dst_ref=dst,
                 send_sem=zsnd_sem.at[stage],
-                recv_sem=zrcv_sem.at[stage],
+                recv_sem=zrcv_sem.at[far_sem if far_sem and is_far(step) else stage],
                 device_id=(peer, me_b),
                 device_id_type=pl.DeviceIdType.MESH,
             ).start()
+
+    def is_far(step):
+        return min(step, groups - step) > groups // 4
 
     def group_wait(part, sem, stage):
         pltpu.make_async_copy(part, part, sem.at[stage]).wait()
@@ -322,15 +325,23 @@
         head = high[:, : 3 * LANES]
         tail = jnp.concatenate([high[:, 3 * LANES :], extra], axis=1)
         wide[stage, me_g] = jnp.concatenate([head, tail], axis=0).astype(BF16)
-        group_send(1 + stage, lambda peer: wide.at[stage, me_g], wide.at[stage, me_g])
+        group_send(1 + stage, lambda peer: wide.at[stage, me_g], wide.at[stage, me_g], 4 + stage)
 
     def summed_groups(stage):
-        group_wait(wide.at[stage, pl.ds(0, groups - 1)], zrcv_sem, 1 + stage)
+        far_steps = [step for step in range(1, groups) if is_far(step)]
+        near_steps = [step for step in range(groups) if not is_far(step)]
         out = jnp.zeros((groups, padded), F32)
-        for g in range(groups):
-            part = wide[stage, g].astype(F32)
-            out = out + jnp.concatenate([part[:groups], part[groups:, : 2 * LANES]], axis=1)
-            extras[stage, g * groups : (g + 1) * groups] = part[groups:, 2 * LANES :]
+        for steps, sem, number in (
+            (near_steps, 1 + stage, len(near_steps) - 1),
+            (far_steps, 4 + stage, len(far_steps)),
+        ):
+            group_wait(wide.at[stage, pl.ds(0, number)], zrcv_sem, sem)
+            for step in steps:
+                g = (me_g + step) % groups
+                part = wide[stage, g].astype(F32)
+                out = out + jnp.concatenate([part[:groups], part[groups:, : 2 * LANES]], axis=1)
+                place = pl.ds(pl.multiple_of(g * groups, groups), groups)
+                extras[stage, place] = part[groups:, 2 * LANES :]
         rest = [extras[stage, pl.ds(c, groups, stride=groups), :] for c in range(groups)]
         scalar = total(rest[tiles] + rest[tiles + 1] + rest[tiles + 2])
         return out + jnp.concatenate(rest[:tiles], axis=1), scalar
@@ -498,7 +509,7 @@
             pltpu.SemaphoreType.DMA((5,)),
             pltpu.SemaphoreType.DMA((5, 2)),
             pltpu.SemaphoreType.DMA((4,)),
-            pltpu.SemaphoreType.DMA((4,)),
+            pltpu.SemaphoreType.DMA((6,)),
         ],
         compiler_params=pltpu.CompilerParams(
             collective_id=0, has_side_effects=True, vmem_limit_bytes=40 * 1024 * 1024

time: 56.2 us -> 56.2 us (level)
  no operation moved by 1% of the time
where the time goes in v6:
time: 56.2 us; the launch traced here: 56.1 us
  Pallas kernels  54.8 us (98%)
  between operations  0.64 us (1%)
  local copies, waits for them, and re-layouts  0.59 us (1%)
    pallas_call x1, Pallas kernels, on_device(): pl.pallas_call(functools.partial(cg_kernel, groups, owners, count, rows,...  54.8 us

profile of v6, /device:TPU:1, one launch (start us, length us, event | category | flops | bytes accessed | tf_op | source)
XLA Modules:
  0.0 56.1 jit_solution(16728774402083262911)
XLA Ops:
  0.6 54.8 %shard_map.77 = f32[2,576]{1,0:T(2,128)S(1)} custom-call(bf16[1536,1152]{1,0:T(8,128)(2,1)} %bitcast.1, s32[12]{0:T(128)} %dest_hbm.1, s32[12]{0:T(128)} %other_hbm.1, s32[12]{0:T(128)} %live_hbm.1, f32[1,576]{1,0:T(1,128)} %damp_hbm.1, f32[1,576]{1,0:T(1,128)} %rhs_hbm.1), custom_call_target="tpu_custom_call" | custom-call | tf_op jit(solution)/shard_map/pallas_call | solution.py:480
  55.5 0.6 %fusion = (f32[1,576]{1,0:T(1,128)}, f32[1,576]{1,0:T(1,128)}) fusion(f32[2,576]{1,0:T(2,128)S(1)} %shard_map.77), kind=kLoop, calls=%fused_computation | loop fusion | bytes 9216 | tf_op jit(solution)/shard_map/slice | solution.py:520
